TPU v7x, 512 devices: a whole 4x8x8 slice. The times are simulated.
512 devices in a mesh: front: 8 (over x, y_hi), row: 8 (over z), col: 8 (over y_lo, core).
Axes of the slice: x: 4, y: 8 (y_hi: 2, y_lo: 4; y = y_hi * 4 + y_lo), z: 8, core: 2. Of those that a mesh axis runs over, the one named last changes fastest.
Arguments:
- parent_front: bfloat16 [8, 8192, 4096], P('front', 'row', 'col'), may hold values from -3 to 28, as said below
- child_front: bfloat16 [8, 4096, 4096], P('front', 'row', 'col'), may hold values from -2 to 2, as said below
- child_blocks: int32 [8, 16], replicated, may hold values from 0 to 31, as said below
- child_mask: int32 [8, 16, 16], replicated, may hold values from 0 to 1, as said below
Outputs:
- factored_front: float32 [8, 8192, 4096], P('front', 'row', 'col')
Inputs may be any that keep to these rules, and one draw needn't show every extreme that they name: `parent_front`: each parent's matrix is symmetric, and its sum with the extend-add of its two children's masked contributions is positive definite. `child_front`: each child's contribution is symmetric. `child_blocks`: for child c, the tiles a with a % 8 == r map to distinct parent tiles congruent to r modulo 8 that rise with a, and one of them is the last such parent tile. `child_mask`: symmetric in its last two dimensions, with ones on the diagonal.
All inputs are finite; a program needn't handle non-finite values.
Results may differ from a plain program's by a relative error of at most 0.0003.
Values may be sent and summed in bfloat16 or wider, within the bound.
No kernel may reach another device: no remote copies, remote signals or barrier semaphores. Data moves between devices by JAX's collectives and lax.ppermute only.
A program may use at most 64 MiB of HBM per device.

v0:
```python
import jax
import jax.numpy as jnp
from jax import lax
from jax.sharding import PartitionSpec as P

B = 256
PANELS = 2


def broadcast(block, axis, owner):
    block = jnp.where(lax.axis_index(axis) == owner, block, jnp.zeros_like(block))
    return lax.psum(block, axis)


def partner(block, axis, stride):
    count = lax.axis_size(axis)
    route = []
    for low in range(count):
        high = low | 1 << stride
        if high != low and high < count:
            route += [(low, high), (high, low)]
    return lax.ppermute(block, axis, route)


def extend_child(
    update,
    child_index,
    child_blocks,
    child_mask,
    grid_row,
    grid_col,
    half_index,
    row_slots,
    col_slots,
):
    row_count = lax.axis_size("row")
    col_count = lax.axis_size("col")
    crow_slots = update.shape[0] // B
    ccol_slots = update.shape[1] // B
    block_map = lax.dynamic_index_in_dim(child_blocks, child_index, 0, keepdims=False)
    tile_mask = lax.dynamic_index_in_dim(child_mask, child_index, 0, keepdims=False)
    map_down = lax.dynamic_index_in_dim(
        block_map.reshape(crow_slots, row_count), grid_row, 1, keepdims=False
    )
    map_across = lax.dynamic_index_in_dim(
        block_map.reshape(ccol_slots, col_count), grid_col, 1, keepdims=False
    )
    mask_band = lax.dynamic_index_in_dim(
        tile_mask.reshape(crow_slots, row_count, tile_mask.shape[1]), grid_row, 1, keepdims=False
    )
    mask_local = lax.dynamic_index_in_dim(
        mask_band.reshape(crow_slots, ccol_slots, col_count), grid_col, 2, keepdims=False
    )
    row_place = (map_down[None, :] // row_count == jnp.arange(row_slots)[:, None]).astype(
        jnp.bfloat16
    )
    col_match = (map_across[None, :] // (2 * col_count) == jnp.arange(col_slots)[:, None]) & (
        (map_across[None, :] // col_count + map_across[None, :]) % 2 == half_index
    )
    col_place = col_match.astype(jnp.bfloat16)
    tile_values = (
        update.reshape(crow_slots, B, ccol_slots, B)
        * mask_local.astype(jnp.bfloat16)[:, None, :, None]
    )
    placed = jnp.einsum(
        "xa,aibj,yb->xiyj", row_place, tile_values, col_place, preferred_element_type=jnp.float32
    )
    return placed.reshape(row_slots * B, col_slots * B)


def factor_column(column, step_index, grid_row, row_count, row_slots):
    first_row = step_index // row_count * B
    pivot_tile = broadcast(column[first_row : first_row + B], "row", step_index % row_count)
    pivot_factor = jnp.linalg.cholesky(pivot_tile)
    solved = lax.linalg.triangular_solve(
        pivot_factor, column, left_side=False, lower=True, transpose_a=True
    )
    block_global = jnp.arange(row_slots) * row_count + grid_row
    shaped = solved.reshape(row_slots, B, B)
    shaped = jnp.where(
        (block_global > step_index)[:, None, None],
        shaped,
        jnp.where((block_global == step_index)[:, None, None], pivot_factor[None], 0.0),
    )
    return shaped.reshape(row_slots * B, B)


def spread_rows(own_rows, step_index, half_index, col_count):
    owner_half = (step_index // col_count + step_index) % 2
    owner_col = step_index % col_count
    along_cols = broadcast(own_rows, "col", owner_col)
    across = partner(along_cols, "front", 0)
    return jnp.where(half_index == owner_half, along_cols, across)


def column_side(row_panel, half_index, grid_col, row_count, col_count, row_slots, col_slots):
    upper_half = (half_index + grid_col) % 2
    root_row = (upper_half * col_count + grid_col) % row_count
    wanted = (
        jnp.arange(col_slots) * (2 * col_count) + upper_half * col_count + grid_col
    ) // row_count
    selector = (wanted[:, None] == jnp.arange(row_slots)[None, :]).astype(jnp.float32)
    chosen = jnp.einsum(
        "ut,tij->uij", selector, row_panel.reshape(row_slots, B, B), precision=lax.Precision.HIGHEST
    )
    return broadcast(chosen.reshape(col_slots * B, B), "row", root_row)


def trailing(slab, row_panel, col_panel, step_index, row_global, col_global):
    product = lax.dot_general(
        row_panel,
        col_panel,
        (((1,), (1,)), ((), ())),
        precision=lax.Precision.HIGHEST,
        preferred_element_type=jnp.float32,
    )
    slot_count = col_global.shape[0]
    slab_blocks = slab.reshape(slab.shape[0], slot_count, B)
    product_blocks = product.reshape(slab.shape[0], slot_count, B)
    row_later = jnp.repeat(row_global > step_index, B)[:, None, None]
    col_later = (col_global > step_index)[None, :, None]
    col_now = (col_global == step_index)[None, :, None]
    merged = jnp.where(
        col_later,
        jnp.where(row_later, slab_blocks - product_blocks, 0.0),
        jnp.where(col_now, row_panel[:, None, :], slab_blocks),
    )
    return merged.reshape(slab.shape)


def on_device(parent_front, child_front, child_blocks, child_mask):
    row_count = lax.axis_size("row")
    col_count = lax.axis_size("col")
    group_index = lax.axis_index("front")
    grid_row = lax.axis_index("row")
    grid_col = lax.axis_index("col")
    half_index = group_index % 2
    sibling = group_index + 1 - 2 * half_index
    local_front = parent_front[0].astype(jnp.float32)
    row_slots = local_front.shape[0] // B
    col_slots = local_front.shape[1] // B
    own_child = child_front[0]
    other_child = partner(own_child, "front", 0)
    local_front = local_front + extend_child(
        own_child,
        group_index,
        child_blocks,
        child_mask,
        grid_row,
        grid_col,
        half_index,
        row_slots,
        col_slots,
    )
    local_front = local_front + extend_child(
        other_child,
        sibling,
        child_blocks,
        child_mask,
        grid_row,
        grid_col,
        half_index,
        row_slots,
        col_slots,
    )
    row_global = jnp.arange(row_slots) * row_count + grid_row
    col_global = (
        jnp.arange(col_slots) * (2 * col_count) + (half_index + grid_col) % 2 * col_count + grid_col
    )
    for step_index in range(PANELS):
        slot_index = step_index // (2 * col_count)
        own_rows = factor_column(
            local_front[:, slot_index * B : (slot_index + 1) * B],
            step_index,
            grid_row,
            row_count,
            row_slots,
        )
        row_panel = spread_rows(own_rows, step_index, half_index, col_count)
        col_panel = column_side(
            row_panel, half_index, grid_col, row_count, col_count, row_slots, col_slots
        )
        local_front = trailing(
            local_front, row_panel, col_panel, step_index, row_global, col_global
        )
    return local_front[None]


def solution(mesh):
    return jax.shard_map(
        on_device,
        mesh=mesh,
        in_specs=(P("front", "row", "col"), P("front", "row", "col"), P(), P()),
        out_specs=P("front", "row", "col"),
        check_vma=False,
    )
```

profile of v0, /device:TPU:2, one launch (start us, length us, event | category | flops | bytes accessed | tf_op | source)
XLA Modules:
  0.0 817.8 jit_solution(14027624428790879510)
XLA Ops:
  6.5 7.7 collective-permute-start
  19.6 2.3 convolution_bitcast_fusion.1
  22.6 3.2 copy.21
  28.0 9.0 %collective-permute-done = bf16[512,512]{1,0:T(8,128)(2,1)} collective-permute-done((bf16[512,512]{1,0:T(8,128)(2,1)}, bf16[512,512]{1,0:T(8,128)(2,1)}, u32[]{:S(2)}, u32[]{:S(2)}) %collective-permute-start) | collective-permute-done | bytes 524320 | tf_op jit(solution)/shard_map/ppermute | solution.py:22
  40.8 2.3 convolution_bitcast_fusion
  43.1 4.1 copy.22
  52.7 83.7 %all-reduce.8.cloned.1.call-done = f32[256,256]{0,1:T(8,128)} async-done(((f32[256,256]{0,1:T(8,128)}), f32[256,256]{0,1:T(8,128)}) %all-reduce.8.cloned.1.call-update) | async-done | bytes 262160 | tf_op jit(solution)/shard_map/psum | solution.py:12
  138.5 11.7 %cholesky.130 = f32[128,128]{1,0:T(8,128)S(1)} custom-call(f32[128,128]{1,0:T(8,128)S(1)} %cholesky.194), custom_call_target="Cholesky" | custom-call | tf_op jit(solution)/shard_map/jit(cholesky)/cholesky | solution.py:74
  150.9 9.8 %custom-call.13 = f32[1,128,128]{1,2,0:T(8,128)S(1)} custom-call(f32[1,128,128]{2,1,0:T(8,128)S(1)} %get-tuple-element.62), custom_call_target="InvertDiagBlocksLowerTriangular" | custom-call | tf_op jit(solution)/shard_map/jit(cholesky)/cholesky | solution.py:74
  161.2 11.7 %cholesky.147 = f32[128,128]{1,0:T(8,128)S(1)} custom-call(f32[128,128]{1,0:T(8,128)S(1)} %convolution_subtract_fusion.2), custom_call_target="Cholesky" | custom-call | tf_op jit(solution)/shard_map/jit(cholesky)/cholesky | solution.py:74
  175.2 4.2 while.4
  179.9 19.7 %custom-call.14 = f32[2,128,128]{1,2,0:T(8,128)S(1)} custom-call(f32[2,128,128]{2,1,0:T(8,128)S(1)} %get-tuple-element.21), custom_call_target="InvertDiagBlocksLowerTriangular" | custom-call | tf_op jit(solution)/shard_map/triangular_solve/custom-call.0 | solution.py:75
  205.2 77.4 %all-reduce.10.cloned.1.call-done = f32[1024,256]{0,1:T(8,128)} async-done(((f32[1024,256]{0,1:T(8,128)}), f32[1024,256]{0,1:T(8,128)}) %all-reduce.10.cloned.1.call-update) | async-done | bytes 1048592 | tf_op jit(solution)/shard_map/psum | solution.py:12
  282.6 5.5 collective-permute-start.1
  288.2 45.9 %collective-permute-done.1 = f32[1024,256]{0,1:T(8,128)} collective-permute-done((f32[1024,256]{0,1:T(8,128)}, f32[1024,256]{0,1:T(8,128)}, u32[]{:S(2)}, u32[]{:S(2)}) %collective-permute-start.1) | collective-permute-done | bytes 1048608 | tf_op jit(solution)/shard_map/ppermute | solution.py:22
  342.7 79.3 %all-reduce.12.cloned.1.call-done = f32[512,256]{1,0:T(8,128)} async-done(((f32[512,256]{1,0:T(8,128)}), f32[512,256]{1,0:T(8,128)}) %all-reduce.12.cloned.1.call-update) | async-done | bytes 524304 | tf_op jit(solution)/shard_map/psum | solution.py:12
  422.0 5.3 fusion.5
  430.0 76.2 %all-reduce.14.cloned.1.call-done = f32[256,256]{0,1:T(8,128)} async-done(((f32[256,256]{0,1:T(8,128)}), f32[256,256]{0,1:T(8,128)}) %all-reduce.14.cloned.1.call-update) | async-done | bytes 262160 | tf_op jit(solution)/shard_map/psum | solution.py:12
  508.9 11.7 %cholesky.164 = f32[128,128]{1,0:T(8,128)S(1)} custom-call(f32[128,128]{1,0:T(8,128)S(1)} %cholesky.197), custom_call_target="Cholesky" | custom-call | tf_op jit(solution)/shard_map/jit(cholesky)/cholesky | solution.py:74
  521.3 9.8 %custom-call.15 = f32[1,128,128]{1,2,0:T(8,128)S(1)} custom-call(f32[1,128,128]{2,1,0:T(8,128)S(1)} %get-tuple-element.58), custom_call_target="InvertDiagBlocksLowerTriangular" | custom-call | tf_op jit(solution)/shard_map/jit(cholesky)/cholesky | solution.py:74
  533.3 11.7 %cholesky.181 = f32[128,128]{1,0:T(8,128)S(1)} custom-call(f32[128,128]{1,0:T(8,128)S(1)} %convolution_subtract_fusion.1), custom_call_target="Cholesky" | custom-call | tf_op jit(solution)/shard_map/jit(cholesky)/cholesky | solution.py:74
  549.6 5.4 while.5
  555.7 20.5 %custom-call.16 = f32[2,128,128]{1,2,0:T(8,128)S(1)} custom-call(f32[2,128,128]{2,1,0:T(8,128)} %copy-done.10), custom_call_target="InvertDiagBlocksLowerTriangular" | custom-call | tf_op jit(solution)/shard_map/triangular_solve/custom-call.0 | solution.py:75
  581.9 77.3 %all-reduce.16.cloned.1.call-done = f32[1024,256]{0,1:T(8,128)} async-done(((f32[1024,256]{0,1:T(8,128)}), f32[1024,256]{0,1:T(8,128)}) %all-reduce.16.cloned.1.call-update) | async-done | bytes 1048592 | tf_op jit(solution)/shard_map/psum | solution.py:12
  659.2 5.5 collective-permute-start.2
  664.7 46.0 %collective-permute-done.2 = f32[1024,256]{0,1:T(8,128)} collective-permute-done((f32[1024,256]{0,1:T(8,128)}, f32[1024,256]{0,1:T(8,128)}, u32[]{:S(2)}, u32[]{:S(2)}) %collective-permute-start.2) | collective-permute-done | bytes 1048608 | tf_op jit(solution)/shard_map/ppermute | solution.py:22
  710.7 2.4 broadcast_select_fusion
  713.1 2.7 reshape.584
  723.6 3.5 reshape.579
  727.1 73.7 %all-reduce.18.cloned.1.call-done = f32[512,256]{1,0:T(8,128)} async-done(((f32[512,256]{1,0:T(8,128)}), f32[512,256]{1,0:T(8,128)}) %all-reduce.18.cloned.1.call-update) | async-done | bytes 524304 | tf_op jit(solution)/shard_map/psum | solution.py:12
  800.9 7.0 fusion.3
  807.9 2.9 copy.36
  (154 shorter events, 70.9 us)
Async XLA Ops:
  6.5 129.9 %all-reduce.8.cloned.1.call-start = ((), (), s32[]{:S(2)}) async-start(), calls=%async_computation | async-start | bytes 524288 | tf_op jit(solution)/shard_map/psum | solution.py:12
  6.5 30.5 %collective-permute-start = (bf16[512,512]{1,0:T(8,128)(2,1)}, bf16[512,512]{1,0:T(8,128)(2,1)}, u32[]{:S(2)}, u32[]{:S(2)}) collective-permute-start(bf16[512,512]{1,0:T(8,128)(2,1)} %bitcast.175), channel_id=1, source_target_pairs={{0,64},{64,0},{128,192},{192,128},{256,320},{320,256},{384,448},{4... | collective-permute-start | bytes 1572872 | tf_op jit(solution)/shard_map/ppermute | solution.py:22
  19.5 2.5 copy-start.7
  22.6 26.9 %copy-start.2 = (bf16[1,1024,512]{1,2,0:T(8,128)(2,1)}, bf16[1,1024,512]{1,2,0:T(8,128)(2,1)S(1)}, u32[]{:S(2)}) copy-start(bf16[1,1024,512]{1,2,0:T(8,128)(2,1)S(1)} %copy.20) | copy-start | bytes 3145732
  47.3 2.2 copy-start.4
  50.2 1.3 copy-start.1
  52.3 230.3 %all-reduce.10.cloned.1.call-start = ((), (), s32[]{:S(2)}) async-start(), calls=%async_computation.1 | async-start | bytes 2097152 | tf_op jit(solution)/shard_map/psum | solution.py:12
  179.4 0.6 copy-start.17
  205.2 216.8 %all-reduce.12.cloned.1.call-start = ((), (), s32[]{:S(2)}) async-start(), calls=%async_computation.2 | async-start | bytes 1048576 | tf_op jit(solution)/shard_map/psum | solution.py:12
  282.6 51.5 %collective-permute-start.1 = (f32[1024,256]{0,1:T(8,128)}, f32[1024,256]{0,1:T(8,128)}, u32[]{:S(2)}, u32[]{:S(2)}) collective-permute-start(f32[1024,256]{0,1:T(8,128)} %all-reduce.10.cloned.1.call-done), channel_id=1, source_target_pairs={{0,64},{64,0},{128,192},{192,128},{256,320},{320,256},{384,448},{4... | collective-permute-start | bytes 3145736 | tf_op jit(solution)/shard_map/ppermute | solution.py:22
  342.4 163.7 %all-reduce.14.cloned.1.call-start = ((), (), s32[]{:S(2)}) async-start(), calls=%async_computation.3 | async-start | bytes 524288 | tf_op jit(solution)/shard_map/psum | solution.py:12
  342.6 84.7 %copy-start.11 = (pred[512]{0:T(512)(128)(4,1)}, pred[512]{0:T(512)(128)(4,1)S(1)}, u32[]{:S(2)}) copy-start(pred[512]{0:T(512)(128)(4,1)S(1)} %broadcast_in_dim.217) | copy-start | bytes 1540
  342.7 84.6 %copy-start.13 = (pred[512]{0:T(512)(128)(4,1)}, pred[512]{0:T(512)(128)(4,1)S(1)}, u32[]{:S(2)}) copy-start(pred[512]{0:T(512)(128)(4,1)S(1)} %broadcast_in_dim.199) | copy-start | bytes 1540
  427.3 1.3 copy-start.5
  429.3 229.9 %all-reduce.16.cloned.1.call-start = ((), (), s32[]{:S(2)}) async-start(), calls=%async_computation.4 | async-start | bytes 2097152 | tf_op jit(solution)/shard_map/psum | solution.py:12
  508.2 0.7 copy-start.9
  545.1 2.0 copy-start.8
  555.0 0.7 copy-start.10
  576.2 4.0 copy-start.6
  581.8 219.0 %all-reduce.18.cloned.1.call-start = ((), (), s32[]{:S(2)}) async-start(), calls=%async_computation.5 | async-start | bytes 1048576 | tf_op jit(solution)/shard_map/psum | solution.py:12
  659.2 51.5 %collective-permute-start.2 = (f32[1024,256]{0,1:T(8,128)}, f32[1024,256]{0,1:T(8,128)}, u32[]{:S(2)}, u32[]{:S(2)}) collective-permute-start(f32[1024,256]{0,1:T(8,128)} %all-reduce.16.cloned.1.call-done), channel_id=1, source_target_pairs={{0,64},{64,0},{128,192},{192,128},{256,320},{320,256},{384,448},{4... | collective-permute-start | bytes 3145736 | tf_op jit(solution)/shard_map/ppermute | solution.py:22
  721.3 2.1 copy-start.16
  721.3 2.2 copy-start.15
  723.6 77.2 %copy-start = (f32[1024,256]{0,1:T(8,128)S(1)}, f32[1024,256]{0,1:T(8,128)}, u32[]{:S(2)}) copy-start(f32[1024,256]{0,1:T(8,128)} %broadcast_select_fusion) | copy-start | bytes 3145732
  723.6 77.2 %copy-start.3 = (bf16[1,1024,512]{1,2,0:T(8,128)(2,1)S(1)}, bf16[1,1024,512]{1,2,0:T(8,128)(2,1)}, u32[]{:S(2)}) copy-start(bf16[1,1024,512]{1,2,0:T(8,128)(2,1)} %copy-done.2) | copy-start | bytes 3145732
  723.6 77.2 %copy-start.12 = (pred[512]{0:T(512)(128)(4,1)S(1)}, pred[512]{0:T(512)(128)(4,1)}, u32[]{:S(2)}) copy-start(pred[512]{0:T(512)(128)(4,1)} %copy-done.11) | copy-start | bytes 1540
  723.6 77.2 %copy-start.14 = (pred[512]{0:T(512)(128)(4,1)S(1)}, pred[512]{0:T(512)(128)(4,1)}, u32[]{:S(2)}) copy-start(pred[512]{0:T(512)(128)(4,1)} %copy-done.13) | copy-start | bytes 1540
Sparse Core Ops, SparseCore 0:
  52.4 83.9 all-reduce.7
  205.3 77.2 all-reduce.9
  342.6 79.3 all-reduce.11
  429.5 76.6 all-reduce.13
  582.0 77.2 all-reduce.15
  721.4 79.3 all-reduce.17
where the time goes:
time: 824 us; the launch traced here: 818 us
  waiting for transfers between devices  569 us (69%)
  other arithmetic  122 us (15%)
  local copies, waits for them, and re-layouts  55.5 us (7%)
  matrix products  34.8 us (4%)
  starting transfers between devices  19.5 us (2%)
  between operations  16.8 us (2%)
    psum x6, waiting for transfers between devices, broadcast(): return lax.psum(block, axis)  468 us
    ppermute x3, waiting for transfers between devices, partner(): return lax.ppermute(block, axis, route)  101 us
    another operation x14, other arithmetic, factor_column(): pivot_factor = jnp.linalg.cholesky(pivot_tile)  69.3 us
    another operation x5, other arithmetic, factor_column(): lax.linalg.triangular_solve(pivot_factor, column, left_side=False, lower=...  40.9 us
    ppermute x3, starting transfers between devices, partner(): return lax.ppermute(block, axis, route)  18.7 us
  transfers between devices with their start and end apart: 9, of which 9 were waited for; matrix products, arithmetic and copies ran while one was open for 2% of the time, Pallas kernels for 0%

commit v1 on v0

--- a/solution.py
+++ b/solution.py
@@ -9,7 +9,7 @@
 
 def broadcast(block, axis, owner):
     block = jnp.where(lax.axis_index(axis) == owner, block, jnp.zeros_like(block))
-    return lax.psum(block, axis)
+    return jnp.sum(lax.all_gather(block, axis), axis=0)
 
 
 def partner(block, axis, stride):

time: 824 us -> 772 us (0.937)
  the two profiles are of different devices: /device:TPU:2 before, /device:TPU:1 now
where the time goes in v1:
time: 772 us; the launch traced here: 764 us
  waiting for transfers between devices  488 us (63%)
  other arithmetic  132 us (17%)
  local copies, waits for them, and re-layouts  68.9 us (9%)
  matrix products  24.6 us (3%)
  starting transfers between devices  23.2 us (3%)
  between operations  16.9 us (2%)
  loops' own time  11 us (1%)
    all_gather x6, waiting for transfers between devices, broadcast(): return jnp.sum(lax.all_gather(block, axis), axis=0)  407 us
    ppermute x3, waiting for transfers between devices, partner(): return lax.ppermute(block, axis, route)  80.7 us
    another operation x14, other arithmetic, factor_column(): pivot_factor = jnp.linalg.cholesky(pivot_tile)  69.3 us
    another operation x5, other arithmetic, factor_column(): lax.linalg.triangular_solve(pivot_factor, column, left_side=False, lower=...  41 us
    unnamed x30, local copies, waits for them, and re-layouts  27.4 us
    ppermute x3, starting transfers between devices, partner(): return lax.ppermute(block, axis, route)  22.2 us
  transfers between devices with their start and end apart: 9, of which 9 were waited for; matrix products, arithmetic and copies ran while one was open for 3% of the time, Pallas kernels for 0%

profile of v1, /device:TPU:1, one launch (start us, length us, event | category | flops | bytes accessed | tf_op | source)
XLA Modules:
  0.0 764.4 jit_solution(6530106720673817399)
XLA Ops:
  6.5 8.3 %collective-permute-start = (bf16[512,512]{1,0:T(8,128)(2,1)}, bf16[512,512]{1,0:T(8,128)(2,1)S(1)}, u32[]{:S(2)}, u32[]{:S(2)}) collective-permute-start(bf16[512,512]{1,0:T(8,128)(2,1)} %bitcast.180), channel_id=1, source_target_pairs={{0,64},{64,0},{128,192},{192,128},{256,320},{320,256},{384,448},{4... | collective-permute-start | bytes 1572872 | tf_op jit(solution)/shard_map/ppermute | solution.py:22
  23.0 6.5 collective-permute-done
  37.6 53.7 %all-gather.15.cloned.1.call-done = f32[2048,256]{1,0:T(8,128)} async-done(((f32[256,256]{1,0:T(8,128)}), f32[2048,256]{1,0:T(8,128)}) %all-gather.15.cloned.1.call-update) | async-done | bytes 2097168 | tf_op jit(solution)/shard_map/all_gather | solution.py:12
  93.2 11.7 %cholesky.130 = f32[128,128]{1,0:T(8,128)S(1)} custom-call(f32[128,128]{1,0:T(8,128)S(1)} %cholesky.194), custom_call_target="Cholesky" | custom-call | tf_op jit(solution)/shard_map/jit(cholesky)/cholesky | solution.py:74
  105.0 9.8 %custom-call.13 = f32[1,128,128]{1,2,0:T(8,128)S(1)} custom-call(f32[1,128,128]{2,1,0:T(8,128)S(1)} %get-tuple-element.62), custom_call_target="InvertDiagBlocksLowerTriangular" | custom-call | tf_op jit(solution)/shard_map/jit(cholesky)/cholesky | solution.py:74
  115.3 11.7 %cholesky.147 = f32[128,128]{1,0:T(8,128)S(1)} custom-call(f32[128,128]{1,0:T(8,128)S(1)} %convolution_subtract_fusion.3), custom_call_target="Cholesky" | custom-call | tf_op jit(solution)/shard_map/jit(cholesky)/cholesky | solution.py:74
  130.8 15.8 %while.4 = (s32[]{:T(128)}, f32[256,256]{1,0:T(8,128)S(1)}, s32[2,2]{1,0:T(2,128)}, f32[2,128,128]{2,1,0:T(8,128)S(1)}, s32[]{:T(128)}) while((s32[]{:T(128)}, f32[256,256]{1,0:T(8,128)S(1)}, s32[2,2]{1,0:T(2,128)}, f32[2,128,128]{2,1,0:T(8,128)S(1)}, s32[]{:T(128)}) %tuple.56), condition=%wide.while_cond, body=%wide.while_body.sunk | while | flops 2 | bytes 131181 | solution.py:75
  147.3 20.5 %custom-call.14 = f32[2,128,128]{1,2,0:T(8,128)S(1)} custom-call(f32[2,128,128]{2,1,0:T(8,128)} %copy-done.8), custom_call_target="InvertDiagBlocksLowerTriangular" | custom-call | tf_op jit(solution)/shard_map/triangular_solve/custom-call.0 | solution.py:75
  171.3 96.8 %all-gather.17.cloned.1.call-done = f32[8192,256]{0,1:T(8,128)} async-done(((f32[1024,256]{0,1:T(8,128)}), f32[8192,256]{0,1:T(8,128)}) %all-gather.17.cloned.1.call-update) | async-done | bytes 8388624 | tf_op jit(solution)/shard_map/all_gather | solution.py:12
  268.1 10.9 %copy.72 = f32[32,8,8,1024]{3,2,1,0:T(8,128)S(1)} copy(f32[32,8,8,1024]{3,1,2,0:T(8,128)} %bitcast.160) | data formatting | bytes 16777216
  281.1 7.0 collective-permute-start.1
  288.1 37.1 %collective-permute-done.1 = f32[1024,256]{0,1:T(8,128)S(1)} collective-permute-done((f32[1024,256]{0,1:T(8,128)S(1)}, f32[1024,256]{0,1:T(8,128)S(1)}, u32[]{:S(2)}, u32[]{:S(2)}) %collective-permute-start.1) | collective-permute-done | bytes 1048608 | tf_op jit(solution)/shard_map/ppermute | solution.py:22
  332.6 2.6 copy.62
  335.2 3.1 copy.38
  340.0 3.0 copy.41
  342.9 55.4 %all-gather.11.cloned.1.call-done = f32[8,512,256]{2,1,0:T(8,128)} async-done(((f32[1,512,256]{2,1,0:T(8,128)}), f32[8,512,256]{2,1,0:T(8,128)}) %all-gather.11.cloned.1.call-update) | async-done | bytes 4194320 | tf_op jit(solution)/shard_map/all_gather | solution.py:12
  398.3 3.3 reduce_sum.56
  401.6 5.2 select_select_fusion.1
  409.5 37.1 %all-gather.19.cloned.1.call-done = f32[2048,256]{1,0:T(8,128)} async-done(((f32[256,256]{1,0:T(8,128)}), f32[2048,256]{1,0:T(8,128)}) %all-gather.19.cloned.1.call-update) | async-done | bytes 2097168 | tf_op jit(solution)/shard_map/all_gather | solution.py:12
  448.6 11.7 %cholesky.164 = f32[128,128]{1,0:T(8,128)S(1)} custom-call(f32[128,128]{1,0:T(8,128)S(1)} %cholesky.197), custom_call_target="Cholesky" | custom-call | tf_op jit(solution)/shard_map/jit(cholesky)/cholesky | solution.py:74
  460.3 9.8 %custom-call.15 = f32[1,128,128]{1,2,0:T(8,128)S(1)} custom-call(f32[1,128,128]{2,1,0:T(8,128)S(1)} %get-tuple-element.58), custom_call_target="InvertDiagBlocksLowerTriangular" | custom-call | tf_op jit(solution)/shard_map/jit(cholesky)/cholesky | solution.py:74
  470.6 11.7 %cholesky.181 = f32[128,128]{1,0:T(8,128)S(1)} custom-call(f32[128,128]{1,0:T(8,128)S(1)} %convolution_subtract_fusion.2), custom_call_target="Cholesky" | custom-call | tf_op jit(solution)/shard_map/jit(cholesky)/cholesky | solution.py:74
  485.6 5.5 while.5
  491.7 20.5 %custom-call.16 = f32[2,128,128]{1,2,0:T(8,128)S(1)} custom-call(f32[2,128,128]{2,1,0:T(8,128)} %copy-done.9), custom_call_target="InvertDiagBlocksLowerTriangular" | custom-call | tf_op jit(solution)/shard_map/triangular_solve/custom-call.0 | solution.py:75
  516.8 96.8 %all-gather.21.cloned.1.call-done = f32[8192,256]{0,1:T(8,128)} async-done(((f32[1024,256]{0,1:T(8,128)}), f32[8192,256]{0,1:T(8,128)}) %all-gather.21.cloned.1.call-update) | async-done | bytes 8388624 | tf_op jit(solution)/shard_map/all_gather | solution.py:12
  613.5 10.9 %copy.74 = f32[32,8,8,1024]{3,2,1,0:T(8,128)S(1)} copy(f32[32,8,8,1024]{3,1,2,0:T(8,128)} %bitcast.161) | data formatting | bytes 16777216
  626.6 7.0 collective-permute-start.2
  633.6 37.1 %collective-permute-done.2 = f32[1024,256]{0,1:T(8,128)} collective-permute-done((f32[1024,256]{0,1:T(8,128)S(1)}, f32[1024,256]{0,1:T(8,128)}, u32[]{:S(2)}, u32[]{:S(2)}) %collective-permute-start.2) | collective-permute-done | bytes 1048608 | tf_op jit(solution)/shard_map/ppermute | solution.py:22
  679.0 67.7 %all-gather.13.cloned.1.call-done = f32[8,512,256]{2,1,0:T(8,128)} async-done(((f32[1,512,256]{2,1,0:T(8,128)}), f32[8,512,256]{2,1,0:T(8,128)}) %all-gather.13.cloned.1.call-update) | async-done | bytes 4194320 | tf_op jit(solution)/shard_map/all_gather | solution.py:12
  746.7 3.3 reduce_sum.59
  750.0 4.5 select_select_fusion
  754.4 2.9 copy.55
  (147 shorter events, 69.2 us)
Async XLA Ops:
  6.5 84.7 %all-gather.15.cloned.1.call-start = ((), (), s32[]{:S(2)}) async-start(), calls=%async_computation.2 | async-start | bytes 2359296 | tf_op jit(solution)/shard_map/all_gather | solution.py:12
  6.5 22.9 %collective-permute-start = (bf16[512,512]{1,0:T(8,128)(2,1)}, bf16[512,512]{1,0:T(8,128)(2,1)S(1)}, u32[]{:S(2)}, u32[]{:S(2)}) collective-permute-start(bf16[512,512]{1,0:T(8,128)(2,1)} %bitcast.180), channel_id=1, source_target_pairs={{0,64},{64,0},{128,192},{192,128},{256,320},{320,256},{384,448},{4... | collective-permute-start | bytes 1572872 | tf_op jit(solution)/shard_map/ppermute | solution.py:22
  20.6 1.6 copy-start
  31.4 1.6 copy-start.2
  33.0 1.2 copy-start.6
  34.9 1.4 copy-start.4
  37.0 231.1 %all-gather.17.cloned.1.call-start = ((), (), s32[]{:S(2)}) async-start(), calls=%async_computation.3 | async-start | bytes 9437184 | tf_op jit(solution)/shard_map/all_gather | solution.py:12
  129.7 38.0 %copy-start.5 = (f32[1024,512]{1,0:T(8,128)S(1)}, f32[1024,512]{1,0:T(8,128)}, u32[]{:S(2)}) copy-start(f32[1024,512]{1,0:T(8,128)} %copy-done.4) | copy-start | bytes 6291460
  146.6 0.7 copy-start.8
  171.3 227.0 %all-gather.11.cloned.1.call-start = ((), (), s32[]{:S(2)}) async-start(), calls=%async_computation | async-start | bytes 4718592 | tf_op jit(solution)/shard_map/all_gather | solution.py:12
  281.1 44.1 %collective-permute-start.1 = (f32[1024,256]{0,1:T(8,128)S(1)}, f32[1024,256]{0,1:T(8,128)S(1)}, u32[]{:S(2)}, u32[]{:S(2)}) collective-permute-start(f32[1024,256]{0,1:T(8,128)S(1)} %bitcast_reduce_fusion.1), channel_id=1, source_target_pairs={{0,64},{64,0},{128,192},{192,128},{256,320},{320,256},{384,448},{4... | collective-permute-start | bytes 3145736 | tf_op jit(solution)/shard_map/ppermute | solution.py:22
  327.3 3.4 copy-start.1
  330.7 115.9 %all-gather.19.cloned.1.call-start = ((), (), s32[]{:S(2)}) async-start(), calls=%async_computation.4 | async-start | bytes 2359296 | tf_op jit(solution)/shard_map/all_gather | solution.py:12
  335.2 3.1 copy-start.3
  407.8 205.8 %all-gather.21.cloned.1.call-start = ((), (), s32[]{:S(2)}) async-start(), calls=%async_computation.5 | async-start | bytes 9437184 | tf_op jit(solution)/shard_map/all_gather | solution.py:12
  491.1 0.6 copy-start.9
  516.7 229.9 %all-gather.13.cloned.1.call-start = ((), (), s32[]{:S(2)}) async-start(), calls=%async_computation.1 | async-start | bytes 4718592 | tf_op jit(solution)/shard_map/all_gather | solution.py:12
  626.6 7.0 copy-start.7
  626.6 44.1 %collective-permute-start.2 = (f32[1024,256]{0,1:T(8,128)S(1)}, f32[1024,256]{0,1:T(8,128)}, u32[]{:S(2)}, u32[]{:S(2)}) collective-permute-start(f32[1024,256]{0,1:T(8,128)S(1)} %bitcast_reduce_fusion), channel_id=1, source_target_pairs={{0,64},{64,0},{128,192},{192,128},{256,320},{320,256},{384,448},{4... | collective-permute-start | bytes 3145736 | tf_op jit(solution)/shard_map/ppermute | solution.py:22
  679.0 71.0 %copy-start.10 = (pred[2]{0:T(512)(128)(4,1)S(1)}, pred[2]{0:T(512)(128)(4,1)}, u32[]{:S(2)}) copy-start(pred[2]{0:T(512)(128)(4,1)} %get-tuple-element.45) | copy-start | bytes 10
Sparse Core Ops, SparseCore 0:
  37.1 54.1 all-gather.14
  171.4 96.6 all-gather.16
  330.8 67.4 all-gather.10
  407.9 38.6 all-gather.18
  516.9 96.6 all-gather.20
  679.1 67.5 all-gather.12
